TPU v7x, 32 devices: a whole 2x2x4 slice. The times are simulated.
32 devices in a mesh: dp: 4 (over y, x), ctx: 2 (over core), head: 4 (over z).
Axes of the slice: x: 2, y: 2, z: 4, core: 2. Of those that a mesh axis runs over, the one named last changes fastest.
Arguments:
- token_values: bfloat16 [4, 1024, 8192], P('dp', 'ctx', 'head'), may hold values from -6 to 6
- gate_values: bfloat16 [4, 1024, 8192], P('dp', 'ctx', 'head'), may hold values from -6 to 6
- state_maps: bfloat16 [4, 1024, 8, 512], P('dp', 'ctx', 'head'), may hold values from -6 to 6
- step_raw: bfloat16 [4, 1024, 128], P('dp', 'ctx', 'head'), may hold values from -6.7 to 2.458448
- log_rate: float32 [128], P('head'), may hold values from -6 to 3
- skip_gain: float32 [128], P('head'), may hold values from 0.5 to 1.5
- conv_values: float32 [4, 8192], P(None, 'head'), may hold values from -3 to 3
- conv_maps: float32 [4, 8, 512], P(None, 'head'), may hold values from -3 to 3
- piece_shift: int32 [32], replicated, may hold values from 0 to 7, as said below
- doc_start: int32 [4, 1024], P('dp', 'ctx'), may hold values 0 or 1
- norm_gain: float32 [8192], P('head'), may hold values from 0.1 to 1.9
- out_weight: bfloat16 [8192, 4096], P('head'), may hold values from -0.0625 to 0.0625
Outputs:
- mixed: bfloat16 [4, 1024, 4096], P('dp', 'ctx', 'head')
Inputs may be any that keep to these rules, and one draw needn't show every extreme that they name: `piece_shift`: no value occurs more than 8 times and some value occurs exactly 8 times.
All inputs are finite; a program needn't handle non-finite values. No bound on the sum of `doc_start` on one device may be relied on, other than what follows from the above.
Results may differ from a plain program's by a relative error of at most 0.014.
Values may be sent and summed in bfloat16 or wider, within the bound.
A program may use at most 256 MiB of HBM per device.

v0:
```python
import jax
import jax.numpy as jnp
from jax import lax
from jax.sharding import PartitionSpec as P

BLOCK_LEN = 128


eps = 1e-05


def passed_along(block, axis, distance):
    devices = range(lax.axis_size(axis))
    route = [(i - distance, i) for i in devices if i - distance in devices]
    return lax.ppermute(block, axis, route)


def prefix(shard, axis, join, neutral):
    place = lax.axis_index(axis)
    gathered = jax.tree.map(
        lambda a, kind: lax.all_gather(a.astype(kind), axis),
        shard,
        jax.tree.map(lambda a: jnp.bfloat16 if a.dtype == jnp.float32 else a.dtype, shard),
    )
    state = jax.tree.map(lambda a, e: jnp.zeros_like(a) + jnp.asarray(e, a.dtype), shard, neutral)

    def one(turn, state):
        return join(
            state,
            jax.tree.map(
                lambda a, own: lax.dynamic_index_in_dim(a, turn, 0, False).astype(own.dtype),
                gathered,
                shard,
            ),
        )

    return lax.fori_loop(0, place, one, state)


def conv_core(ext_values, weight, free_ext, length):
    tap_count = weight.shape[0]
    summed = jnp.zeros((length,) + ext_values.shape[1:], jnp.float32)
    keeping = jnp.ones((length,), jnp.float32)
    bshape = (length,) + (1,) * (ext_values.ndim - 1)
    for back in range(tap_count):
        if back > 0:
            keeping = keeping * free_ext[tap_count - back : tap_count - back + length]
        sample = ext_values[tap_count - 1 - back : tap_count - 1 - back + length].astype(
            jnp.float32
        )
        summed = summed + weight[tap_count - 1 - back] * sample * keeping.reshape(bshape)
    return jax.nn.silu(summed).astype(jnp.bfloat16)


def body(
    token_values,
    gate_values,
    state_maps,
    step_raw,
    log_rate,
    skip_gain,
    conv_values,
    conv_maps,
    piece_shift,
    doc_start,
    norm_gain,
    out_weight,
):
    owners = lax.axis_size(("dp", "ctx"))
    myself = lax.axis_index(("dp", "ctx"))
    slots = piece_shift.shape[0]
    rows = token_values.shape[1]
    piece_rows = rows // slots
    most = 2 * slots // owners
    slot_ids = jnp.arange(slots, dtype=jnp.int32)
    matching = piece_shift[:, None] == piece_shift[None, :]
    ranking = jnp.sum(
        (matching & (slot_ids[None, :] < slot_ids[:, None])).astype(jnp.int32), axis=1
    )
    offsets = (jnp.arange(owners, dtype=jnp.int32) - myself) % owners
    chosen = (piece_shift[None, None, :] == offsets[:, None, None]) & (
        ranking[None, None, :] == jnp.arange(most, dtype=jnp.int32)[None, :, None]
    )
    send_slot = jnp.sum(chosen.astype(jnp.int32) * slot_ids[None, None, :], axis=2)

    def outgoing(local):
        pieces = local[0].reshape((slots, piece_rows) + local.shape[2:])
        return pieces[send_slot]

    incoming = (
        lax.all_to_all(
            outgoing(token_values), ("dp", "ctx"), split_axis=0, concat_axis=0, tiled=True
        ),
        lax.all_to_all(
            outgoing(gate_values), ("dp", "ctx"), split_axis=0, concat_axis=0, tiled=True
        ),
        lax.all_to_all(
            outgoing(state_maps), ("dp", "ctx"), split_axis=0, concat_axis=0, tiled=True
        ),
        lax.all_to_all(outgoing(step_raw), ("dp", "ctx"), split_axis=0, concat_axis=0, tiled=True),
    )
    source = (myself - piece_shift) % owners

    def placed(received):
        return received[source, ranking].reshape((rows,) + received.shape[3:])

    x_pack = placed(incoming[0])
    z_pack = placed(incoming[1])
    map_pack = placed(incoming[2])
    dt_pack = placed(incoming[3])
    margin = conv_values.shape[0] - 1
    flags = doc_start[0].astype(jnp.bfloat16)
    rim_x, rim_maps, rim_flags = passed_along(
        (x_pack[rows - margin :], map_pack[rows - margin :], flags[rows - margin :]), "ctx", 1
    )
    free_ext = 1.0 - jnp.concatenate([rim_flags, flags]).astype(jnp.float32)
    x_conv = conv_core(jnp.concatenate([rim_x, x_pack]), conv_values, free_ext, rows)
    map_conv = conv_core(jnp.concatenate([rim_maps, map_pack]), conv_maps, free_ext, rows)
    heads_local = log_rate.shape[0]
    groups_local = map_pack.shape[1]
    per_group = heads_local // groups_local
    width = x_pack.shape[1] // heads_local
    state = map_pack.shape[2] // 2
    span = BLOCK_LEN
    blocks = rows // span
    step_dt = jax.nn.softplus(dt_pack.astype(jnp.float32))
    log_decay = step_dt * (-jnp.exp(log_rate))[None, :]
    cum_t = jnp.cumsum(log_decay.reshape(blocks, span, heads_local), axis=1).transpose(0, 2, 1)
    dt_t = step_dt.reshape(blocks, span, heads_local).transpose(0, 2, 1)
    segment = jnp.cumsum(doc_start[0].reshape(blocks, span), axis=1)
    x_blocks = x_conv.reshape(blocks, span, groups_local, per_group, width)
    b_blocks = map_conv[:, :, :state].reshape(blocks, span, groups_local, state)
    c_blocks = map_conv[:, :, state:].reshape(blocks, span, groups_local, state)
    scores = jnp.einsum("bqgn,bsgn->bgqs", c_blocks, b_blocks, preferred_element_type=jnp.float32)
    later = jnp.arange(span)[:, None] >= jnp.arange(span)[None, :]
    allowed = later[None] & (segment[:, :, None] == segment[:, None, :])
    spread = cum_t[:, :, :, None] - cum_t[:, :, None, :]
    decay = jnp.exp(jnp.where(allowed[:, None], spread, -jnp.inf))
    weights = (
        decay.reshape(blocks, groups_local, per_group, span, span)
        * scores[:, :, None]
        * dt_t.reshape(blocks, groups_local, per_group, 1, span)
    ).astype(jnp.bfloat16)
    y_diag = jnp.einsum("bghts,bsghp->btghp", weights, x_blocks, preferred_element_type=jnp.float32)
    same_end = (segment == segment[:, -1:]).astype(jnp.float32)
    carry_coef = jnp.exp(cum_t[:, :, -1:] - cum_t) * dt_t * same_end[:, None, :]
    x_weighted = (
        x_blocks.astype(jnp.float32)
        * carry_coef.transpose(0, 2, 1).reshape(blocks, span, groups_local, per_group, 1)
    ).astype(jnp.bfloat16)
    block_states = jnp.einsum(
        "bsghp,bsgn->bghpn", x_weighted, b_blocks, preferred_element_type=jnp.float32
    ).reshape(blocks, heads_local, width, state)
    block_gates = jnp.exp(cum_t[:, :, -1]) * (segment[:, -1] == 0).astype(jnp.float32)[:, None]

    def advance(carry, item):
        factor, summed = carry
        gate_now, state_now = item
        return ((factor * gate_now, gate_now[:, None, None] * summed + state_now), (factor, summed))

    start_pair = (
        jnp.ones((heads_local,), jnp.float32),
        jnp.zeros((heads_local, width, state), jnp.float32),
    )
    slab_pair, prior_pair = lax.scan(advance, start_pair, (block_gates, block_states))
    prior_gate, prior_state = prior_pair

    def combine(earlier, latter):
        return (earlier[0] * latter[0], latter[0][:, None, None] * earlier[1] + latter[1])

    arriving = prefix(slab_pair, "ctx", combine, start_pair)[1]
    entering = (
        (prior_state + prior_gate[:, :, None, None] * arriving[None])
        .astype(jnp.bfloat16)
        .reshape(blocks, groups_local, per_group, width, state)
    )
    y_off = jnp.einsum("bqgn,bghpn->bqghp", c_blocks, entering, preferred_element_type=jnp.float32)
    reach = (
        (jnp.exp(cum_t) * (segment == 0).astype(jnp.float32)[:, None, :])
        .transpose(0, 2, 1)
        .reshape(blocks, span, groups_local, per_group, 1)
    )
    mixed_y = (
        y_diag
        + y_off * reach
        + skip_gain.reshape(groups_local, per_group, 1) * x_blocks.astype(jnp.float32)
    )
    gated = mixed_y * jax.nn.silu(
        z_pack.astype(jnp.float32).reshape(blocks, span, groups_local, per_group, width)
    )
    power = jnp.mean(gated * gated, axis=(3, 4), keepdims=True)
    normed = (
        (gated * lax.rsqrt(power + eps) * norm_gain.reshape(groups_local, per_group, width))
        .astype(jnp.bfloat16)
        .reshape(rows, heads_local * width)
    )
    partial_value = jnp.dot(normed, out_weight, preferred_element_type=jnp.float32)
    result = lax.psum_scatter(
        partial_value.astype(jnp.bfloat16), "head", scatter_dimension=1, tiled=True
    )
    return result[None]


def solution(mesh):
    return jax.shard_map(
        body,
        mesh=mesh,
        in_specs=(
            P("dp", "ctx", "head"),
            P("dp", "ctx", "head"),
            P("dp", "ctx", "head", None),
            P("dp", "ctx", "head"),
            P("head"),
            P("head"),
            P(None, "head"),
            P(None, "head", None),
            P(),
            P("dp", "ctx"),
            P("head"),
            P("head", None),
        ),
        out_specs=P("dp", "ctx", "head"),
        check_vma=False,
    )
```

profile of v0, /device:TPU:8, one launch (start us, length us, event | category | flops | bytes accessed | tf_op | source)
XLA Modules:
  0.0 307.3 jit_solution(16056378961611927930)
XLA Ops:
  6.5 1.0 convert_reduce_fusion
  8.6 0.9 copy.148
  10.1 0.9 reshape.334
  11.0 3.7 %all-to-all-start.1 = ((bf16[8,2,2048]{2,1,0:T(2,128)(2,1)}), bf16[8,2,2048]{2,1,0:T(2,128)(2,1)S(1)}, u32[]{:S(2)}, u32[]{:S(2)}) async-start(bf16[8,2,2048]{2,1,0:T(2,128)(2,1)} %reshape.334), calls=%async_computation.1 | async-start | bytes 131072 | tf_op jit(solution)/shard_map/all_to_all | solution.py:100
  14.8 1.4 copy.157
  16.2 2.0 gather_fusion.4
  18.2 1.6 all-to-all-done.1
  19.8 4.3 %all-to-all-start.2 = ((bf16[8,8,16,2,512]{4,2,3,1,0:T(8,128)(2,1)}), bf16[8,8,16,2,512]{4,2,3,1,0:T(8,128)(2,1)}, u32[]{:S(2)}, u32[]{:S(2)}) async-start(bf16[8,8,16,2,512]{4,2,3,1,0:T(8,128)(2,1)} %bitcast.108), calls=%async_computation.2 | async-start | bytes 4194304 | tf_op jit(solution)/shard_map/all_to_all | solution.py:97
  24.2 2.7 gather_fusion
  26.9 23.9 %all-to-all-done.2 = bf16[8,8,16,2,512]{4,2,3,1,0:T(8,128)(2,1)} async-done(((bf16[8,8,16,2,512]{4,2,3,1,0:T(8,128)(2,1)}), bf16[8,8,16,2,512]{4,2,3,1,0:T(8,128)(2,1)}, u32[]{:S(2)}, u32[]{:S(2)}) %all-to-all-start.2) | async-done | bytes 2097184 | tf_op jit(solution)/shard_map/all_to_all | solution.py:97
  50.8 4.6 %all-to-all-start = ((bf16[8,8,16,2048]{3,2,1,0:T(8,128)(2,1)}), bf16[8,8,16,2048]{3,2,1,0:T(8,128)(2,1)}, u32[]{:S(2)}, u32[]{:S(2)}) async-start(bf16[8,8,16,2048]{3,2,1,0:T(8,128)(2,1)} %bitcast.104), calls=%async_computation | async-start | bytes 8388608 | tf_op jit(solution)/shard_map/all_to_all | solution.py:91
  55.4 2.3 collective-permute-start.1
  58.1 4.4 %gather_fusion.6 = bf16[64,16,2048]{2,1,0:T(8,128)(2,1)} fusion(bf16[32,16,2048]{2,1,0:T(8,128)(2,1)} %bitcast.109, s32[1024]{0:T(1024)S(1)} %pad_clamp_fusion), kind=kCustom, calls=%fused_computation.6 | custom fusion | bytes 8388864 | tf_op jit(solution)/shard_map/gather | solution.py:88
  68.9 2.2 gather_fusion.5
  71.3 1.3 collective-permute-start.2
  72.6 1.3 broadcast_multiply_fusion.1
  73.9 3.7 %multiply_convert_fusion.4 = bf16[512,2,512]{2,0,1:T(8,128)(2,1)} fusion(bf16[512,2,512]{2,0,1:T(8,128)(2,1)S(1)} %bitcast.113, bf16[3,2,512]{2,0,1:T(4,128)(2,1)S(1)} %collective-permute-done.2, f32[512]{0:T(512)} %get-tuple-element.144, f32[2,512]{1,0:T(2,128)} %get-tuple-element.161, f32[512]{0:T(512)} %get-tuple-element.145, ...), kind=kLoop, calls=%fused_computation.46 | loop fusion | flops 14680064 | bytes 2125824 | tf_op jit(solution)/shard_map/convert_element_type | solution.py:52
  77.6 26.9 %all-to-all-done = bf16[8,8,16,2048]{3,2,1,0:T(8,128)(2,1)} async-done(((bf16[8,8,16,2048]{3,2,1,0:T(8,128)(2,1)}), bf16[8,8,16,2048]{3,2,1,0:T(8,128)(2,1)}, u32[]{:S(2)}, u32[]{:S(2)}) %all-to-all-start) | async-done | bytes 4194336 | tf_op jit(solution)/shard_map/all_to_all | solution.py:91
  104.5 4.6 %all-to-all-start.3 = ((bf16[8,8,16,2048]{3,2,1,0:T(8,128)(2,1)}), bf16[8,8,16,2048]{3,2,1,0:T(8,128)(2,1)}, u32[]{:S(2)}, u32[]{:S(2)}) async-start(bf16[8,8,16,2048]{3,2,1,0:T(8,128)(2,1)} %bitcast.103), calls=%async_computation.3 | async-start | bytes 8388608 | tf_op jit(solution)/shard_map/all_to_all | solution.py:94
  109.1 4.2 %gather_fusion.1 = bf16[32,16,2048]{2,1,0:T(8,128)(2,1)} fusion(bf16[8,8,16,2048]{3,2,1,0:T(8,128)(2,1)} %all-to-all-done, s32[32]{0:T(128)S(1)} %fusion.39), kind=kCustom, calls=%fused_computation.1 | custom fusion | bytes 4194560 | tf_op jit(solution)/shard_map/gather | solution.py:105
  114.1 2.4 collective-permute-start
  116.5 1.3 fusion.42
  117.8 9.0 %multiply_convert_fusion.3 = bf16[512,2048]{1,0:T(8,128)(2,1)} fusion(bf16[512,2048]{1,0:T(8,128)(2,1)} %bitcast.107, bf16[3,2048]{1,0:T(4,128)(2,1)S(1)} %collective-permute-done, f32[512]{0:T(512)} %get-tuple-element.144, f32[2048]{0:T(1024)} %bitcast.129, f32[512]{0:T(512)} %get-tuple-element.145, f32[2048]{0:T(1024)} %bitcast.130, ...), kind=kLoop, calls=%fused_computation.35 | loop fusion | flops 29360128 | bytes 4245504 | tf_op jit(solution)/shard_map/convert_element_type | solution.py:52
  126.8 7.1 %reshape.323 = bf16[4,128,2,16,64]{4,3,2,1,0:T(8,128)(2,1)} reshape(bf16[512,2048]{1,0:T(8,128)(2,1)} %multiply_convert_fusion.3) | data formatting | bytes 4194304 | tf_op jit(solution)/shard_map/reshape | solution.py:131
  133.9 6.5 %copy.161 = bf16[4,128,2,16,64]{1,4,3,2,0:T(8,128)(2,1)} copy(bf16[4,128,2,16,64]{4,3,2,1,0:T(8,128)(2,1)} %reshape.323) | data formatting | bytes 4194304 | tf_op jit(solution)/shard_map/reshape | solution.py:131
  140.4 6.1 %fusion.16 = f32[4,2,16,64,256]{4,3,2,1,0:T(8,128)} fusion(bf16[4,128,2,16,64]{1,4,3,2,0:T(8,128)(2,1)} %copy.161, f32[4,128,2,16]{1,3,2,0:T(8,128)S(1)} %get-tuple-element.152, bf16[4,128,2,256,1]{3,1,0,2,4:T(8,128)(2,1)S(1)} %bitcast.110), kind=kOutput, calls=%fused_computation.41 | convolution fusion | flops 540016640 | bytes 11075584 | tf_op jit(solution)/shard_map/bsghp,bsgn->bghpn/dot_general | solution.py:151
  146.5 17.0 %while.30 = (s32[]{:T(128)}, f32[32]{0:T(128)S(1)}, f32[32,64,256]{2,1,0:T(8,128)S(1)}, f32[4,32]{1,0:T(4,128)S(1)}, f32[4,32,64,256]{3,2,1,0:T(8,128)}, /*index...) while((s32[]{:T(128)}, f32[32]{0:T(128)S(1)}, ...), condition=%wide.region_5.6_spmd.clone, body=%wide.region_4.5_spmd.clone.sunk | while | flops 2097219 | bytes 10487413 | solution.py:165
  147.1 1.6 bitcast_dynamic-update-slice_fusion.2
  148.7 2.0 bitcast_add_fusion.2
  151.4 1.6 bitcast_dynamic-update-slice_fusion.2
  152.9 2.0 bitcast_add_fusion.2
  155.6 1.6 bitcast_dynamic-update-slice_fusion.2
  157.2 2.0 bitcast_add_fusion.2
  159.9 1.6 bitcast_dynamic-update-slice_fusion.2
  161.5 2.0 bitcast_add_fusion.2
  163.5 1.1 convert_element_type.146
  167.7 1.1 fusion.25
  168.8 2.9 gather_fusion.7
  171.7 5.5 %reshape.247 = f32[4,128,2,16,64]{4,3,2,1,0:T(8,128)} reshape(bf16[32,16,2048]{2,1,0:T(8,128)(2,1)S(1)} %gather_fusion.7) | data formatting | bytes 6291456 | tf_op jit(solution)/shard_map/convert_element_type | solution.py:189
  177.2 8.2 %copy.173 = f32[4,128,2,16,64]{1,4,3,2,0:T(8,128)} copy(f32[4,128,2,16,64]{4,3,2,1,0:T(8,128)} %reshape.247) | data formatting | bytes 8388608 | tf_op jit(solution)/shard_map/convert_element_type | solution.py:189
  185.7 2.4 all-reduce
  188.2 6.0 %fusion.3 = f32[4,2,16,64,128]{4,3,2,1,0:T(8,128)} fusion(bf16[4,128,2,16,64]{1,4,3,2,0:T(8,128)(2,1)S(1)} %copy-done.2, f32[4,2,16,128]{3,2,1,0:T(8,128)S(1)} %bitcast.125, f32[4,2,128,128]{3,2,1,0:T(8,128)S(1)} %copy-done.5, f32[4,2,16,128]{3,2,1,0:T(8,128)S(1)} %bitcast.126, pred[4,128,128]{2,1,0:T(8,128)(4,1)S(1)} %copy-done.7), kind=kOutput, calls=%fused_computation.22 | convolution fusion | flops 278921216 | bytes 7012352 | tf_op jit(solution)/shard_map/bghts,bsghp->btghp/dot_general | solution.py:144
  194.7 4.3 %add_convert_fusion = bf16[4,32,64,256]{3,2,1,0:T(8,128)(2,1)S(1)} fusion(f32[4,32,64,256]{3,2,1,0:T(8,128)} %get-tuple-element.89, f32[32,64,256]{2,1,0:T(8,128)S(1)} %get-tuple-element.93, f32[4,32]{1,0:T(4,128)S(1)} %get-tuple-element.90), kind=kLoop, calls=%fused_computation.17 | loop fusion | flops 6291456 | bytes 14680576 | tf_op jit(solution)/shard_map/convert_element_type | solution.py:174
  199.1 0.8 copy-done.4
  199.9 3.8 %multiply_reduce_fusion = (f32[4,128,2]{1,2,0:T(2,128)S(1)}, f32[4,128,2,16,64]{1,4,3,2,0:T(8,128)S(1)}) fusion(f32[4,128,2,16,64]{1,4,3,2,0:T(8,128)S(1)} %copy-done.4, bf16[4,128,2,16,64]{1,4,3,2,0:T(8,128)(2,1)S(1)} %copy-done.3, f32[2,16]{1,0:T(2,128)S(1)} %mul.377, f32[4,128,2,16]{1,3,2,0:T(8,128)S(1)} %copy-done.8, ...), kind=kOutput, calls=%fused_computation.29 | convolution fusion | flops 549452800 | bytes 19468416 | tf_op jit(solution)/shard_map/bqgn,bghpn->bqghp/dot_general | solution.py:177
  204.6 2.0 copy.174
  206.5 14.1 %convolution_convert_fusion = bf16[512,4096]{1,0:T(8,128)(2,1)} fusion(bf16[2048,4096]{1,0:T(8,128)(2,1)} %param.27, bf16[256,8,4,128]{3,2,1,0:T(4,128)(2,1)S(1)} %bitcast.117), kind=kOutput, calls=%fused_computation.19 | convolution fusion | flops 8592031744 | bytes 23068672 | tf_op jit(solution)/shard_map/dot_general | solution.py:197
  220.7 79.7 %reduce-scatter.2.cloned.1.call-done = bf16[512,1024]{1,0:T(8,128)(2,1)} async-done(((bf16[512,4096]{1,0:T(8,128)(2,1)}), bf16[512,1024]{1,0:T(8,128)(2,1)}) %reduce-scatter.2.cloned.1.call-update) | async-done | bytes 1048592 | tf_op jit(solution)/shard_map/reduce_scatter | solution.py:198
  (108 shorter events, 16.2 us)
Async XLA Ops:
  6.5 17.6 %copy-start = (bf16[1,512,2048]{2,1,0:T(8,128)(2,1)S(1)}, bf16[1,512,2048]{2,1,0:T(8,128)(2,1)}, u32[]{:S(2)}) copy-start(bf16[1,512,2048]{2,1,0:T(8,128)(2,1)} %param.16) | copy-start | bytes 6291460
  11.0 8.7 %all-to-all-start.1 = ((bf16[8,2,2048]{2,1,0:T(2,128)(2,1)}), bf16[8,2,2048]{2,1,0:T(2,128)(2,1)S(1)}, u32[]{:S(2)}, u32[]{:S(2)}) async-start(bf16[8,2,2048]{2,1,0:T(2,128)(2,1)} %reshape.334), calls=%async_computation.1 | async-start | bytes 131072 | tf_op jit(solution)/shard_map/all_to_all | solution.py:100
  19.8 31.0 %all-to-all-start.2 = ((bf16[8,8,16,2,512]{4,2,3,1,0:T(8,128)(2,1)}), bf16[8,8,16,2,512]{4,2,3,1,0:T(8,128)(2,1)}, u32[]{:S(2)}, u32[]{:S(2)}) async-start(bf16[8,8,16,2,512]{4,2,3,1,0:T(8,128)(2,1)} %bitcast.108), calls=%async_computation.2 | async-start | bytes 4194304 | tf_op jit(solution)/shard_map/all_to_all | solution.py:97
  24.1 2.8 copy-start.10
  50.8 53.7 %all-to-all-start = ((bf16[8,8,16,2048]{3,2,1,0:T(8,128)(2,1)}), bf16[8,8,16,2048]{3,2,1,0:T(8,128)(2,1)}, u32[]{:S(2)}, u32[]{:S(2)}) async-start(bf16[8,8,16,2048]{3,2,1,0:T(8,128)(2,1)} %bitcast.104), calls=%async_computation | async-start | bytes 8388608 | tf_op jit(solution)/shard_map/all_to_all | solution.py:91
  55.4 9.3 %collective-permute-start.1 = (bf16[3]{0:T(256)(128)(2,1)S(1)}, bf16[3]{0:T(256)(128)(2,1)S(1)}, u32[]{:S(2)}, u32[]{:S(2)}) collective-permute-start(bf16[3]{0:T(256)(128)(2,1)S(1)} %slice_bitcast_fusion.4), channel_id=1, source_target_pairs={{0,4},{1,5},{2,6},{3,7},{8,12},{9,13},{10,14},{11,15},{16,20},{17,... | collective-permute-start | bytes 26 | tf_op jit(solution)/shard_map/ppermute | solution.py:15
  58.1 5.3 %copy-start.16 = (f32[32]{0:T(128)S(1)}, f32[32]{0:T(128)}, u32[]{:S(2)}) copy-start(f32[32]{0:T(128)} %param.20) | copy-start | bytes 388
  58.1 5.4 %copy-start.14 = (s32[32]{0:T(128)S(1)}, s32[32]{0:T(128)}, u32[]{:S(2)}) copy-start(s32[32]{0:T(128)} %param.24) | copy-start | bytes 388
  58.1 5.5 %copy-start.11 = (f32[4,2,512]{2,1,0:T(2,128)S(1)}, f32[4,2,512]{2,1,0:T(2,128)}, u32[]{:S(2)}) copy-start(f32[4,2,512]{2,1,0:T(2,128)} %param.23) | copy-start | bytes 49156
  58.1 6.1 %copy-start.9 = (f32[4,2048]{1,0:T(4,128)S(1)}, f32[4,2048]{1,0:T(4,128)}, u32[]{:S(2)}) copy-start(f32[4,2048]{1,0:T(4,128)} %param.22) | copy-start | bytes 98308
  71.3 2.6 collective-permute-start.2
  104.5 64.3 %all-to-all-start.3 = ((bf16[8,8,16,2048]{3,2,1,0:T(8,128)(2,1)}), bf16[8,8,16,2048]{3,2,1,0:T(8,128)(2,1)}, u32[]{:S(2)}, u32[]{:S(2)}) async-start(bf16[8,8,16,2048]{3,2,1,0:T(8,128)(2,1)} %bitcast.103), calls=%async_computation.3 | async-start | bytes 8388608 | tf_op jit(solution)/shard_map/all_to_all | solution.py:94
  109.1 85.2 %all-gather.4.cloned.1.call-start = ((), (), s32[]{:S(2)}) async-start(), calls=%async_computation.6 | async-start | bytes 3145728 | tf_op jit(solution)/shard_map/all_gather | solution.py:21
  114.1 3.7 %collective-permute-start = (bf16[3,2048]{1,0:T(4,128)(2,1)S(1)}, bf16[3,2048]{1,0:T(4,128)(2,1)S(1)}, u32[]{:S(2)}, u32[]{:S(2)}) collective-permute-start(bf16[3,2048]{1,0:T(4,128)(2,1)S(1)} %slice.121), channel_id=1, source_target_pairs={{0,4},{1,5},{2,6},{3,7},{8,12},{9,13},{10,14},{11,15},{16,20},{17,... | collective-permute-start | bytes 36872 | tf_op jit(solution)/shard_map/ppermute | solution.py:15
  140.4 6.1 %copy-start.12 = (f32[32]{0:T(128)S(1)}, f32[32]{0:T(128)}, u32[]{:S(2)}) copy-start(f32[32]{0:T(128)} %custom-call.8) | copy-start | bytes 388
  140.4 6.1 %copy-start.15 = (f32[4,32]{1,0:T(4,128)S(1)}, f32[4,32]{1,0:T(4,128)}, u32[]{:S(2)}) copy-start(f32[4,32]{1,0:T(4,128)} %custom-call.18) | copy-start | bytes 1540
  163.5 1.2 copy-start.17
  163.5 1.3 copy-start.13
  163.5 1.4 copy-start.18
  164.7 135.7 %reduce-scatter.2.cloned.1.call-start = ((), (), s32[]{:S(2)}) async-start(), calls=%async_computation.5 | async-start | bytes 5242880 | tf_op jit(solution)/shard_map/reduce_scatter | solution.py:198
  177.2 11.0 %copy-start.2 = (bf16[4,128,2,16,64]{1,4,3,2,0:T(8,128)(2,1)S(1)}, bf16[4,128,2,16,64]{1,4,3,2,0:T(8,128)(2,1)}, u32[]{:S(2)}) copy-start(bf16[4,128,2,16,64]{1,4,3,2,0:T(8,128)(2,1)} %copy.161) | copy-start | bytes 6291460
  177.2 11.0 %copy-start.5 = (f32[4,2,128,128]{3,2,1,0:T(8,128)S(1)}, f32[4,2,128,128]{3,2,1,0:T(8,128)}, u32[]{:S(2)}) copy-start(f32[4,2,128,128]{3,2,1,0:T(8,128)} %fusion.25) | copy-start | bytes 1572868
  177.2 11.0 %copy-start.6 = (f32[4,32,128]{2,1,0:T(8,128)S(1)}, f32[4,32,128]{2,1,0:T(8,128)}, u32[]{:S(2)}) copy-start(f32[4,32,128]{2,1,0:T(8,128)} %copy.155) | copy-start | bytes 196612
  177.2 11.0 %copy-start.7 = (pred[4,128,128]{2,1,0:T(8,128)(4,1)S(1)}, pred[4,128,128]{2,1,0:T(8,128)(4,1)}, u32[]{:S(2)}) copy-start(pred[4,128,128]{2,1,0:T(8,128)(4,1)} %compare_and_fusion) | copy-start | bytes 196612
  194.7 4.4 %copy-start.3 = (bf16[4,128,2,16,64]{1,4,3,2,0:T(8,128)(2,1)S(1)}, bf16[4,128,2,16,64]{1,4,3,2,0:T(8,128)(2,1)}, u32[]{:S(2)}) copy-start(bf16[4,128,2,16,64]{1,4,3,2,0:T(8,128)(2,1)} %copy.161) | copy-start | bytes 6291460
  194.7 5.2 %copy-start.4 = (f32[4,128,2,16,64]{1,4,3,2,0:T(8,128)S(1)}, f32[4,128,2,16,64]{1,4,3,2,0:T(8,128)}, u32[]{:S(2)}) copy-start(f32[4,128,2,16,64]{1,4,3,2,0:T(8,128)} %copy.173) | copy-start | bytes 12582916
  194.7 5.2 %copy-start.8 = (f32[4,128,2,16]{1,3,2,0:T(8,128)S(1)}, f32[4,128,2,16]{1,3,2,0:T(8,128)}, u32[]{:S(2)}) copy-start(f32[4,128,2,16]{1,3,2,0:T(8,128)} %get-tuple-element.151) | copy-start | bytes 196612
  206.5 93.9 %copy-start.1 = (bf16[1,512,2048]{2,1,0:T(8,128)(2,1)S(1)}, bf16[1,512,2048]{2,1,0:T(8,128)(2,1)}, u32[]{:S(2)}) copy-start(bf16[1,512,2048]{2,1,0:T(8,128)(2,1)} %param.16) | copy-start | bytes 6291460
Sparse Core Ops, SparseCore 0:
  164.8 12.1 all-gather.3
  220.8 79.5 reduce-scatter.1
where the time goes:
time: 310 us; the launch traced here: 307 us
  waiting for transfers between devices  132 us (43%)
  local copies, waits for them, and re-layouts  60.8 us (20%)
  other arithmetic  42.8 us (14%)
  matrix products  31.2 us (10%)
  starting transfers between devices  23.3 us (8%)
  between operations  14.5 us (5%)
    reduce_scatter x1, waiting for transfers between devices, body(): lax.psum_scatter(partial_value.astype(jnp.bfloat16), 'head', scatter_dime...  79.7 us
    all_to_all x1, waiting for transfers between devices, body(): lax.all_to_all(outgoing(token_values), ('dp', 'ctx'), split_axis=0, conca...  26.9 us
    all_to_all x1, waiting for transfers between devices, body(): lax.all_to_all(outgoing(state_maps), ('dp', 'ctx'), split_axis=0, concat_...  23.9 us
    dot_general x1, matrix products, body(): jnp.dot(normed, out_weight, preferred_element_type=jnp.float32)  14.1 us
    convert_element_type x2, local copies, waits for them, and re-layouts, body(): z_pack.astype(jnp.float32)  13.7 us
    reshape x2, local copies, waits for them, and re-layouts, body(): x_blocks = x_conv.reshape(blocks, span, groups_local, per_group, width)  13.6 us
    convert_element_type x2, other arithmetic, conv_core(): return jax.nn.silu(summed).astype(jnp.bfloat16)  12.7 us
    gather x5, local copies, waits for them, and re-layouts, placed(): return received[source, ranking].reshape((rows,) + received.shape[3:])  10 us
  transfers between devices with their start and end apart: 9, of which 4 were waited for; matrix products, arithmetic and copies ran while one was open for 34% of the time, Pallas kernels for 0%

commit v1 on v0

v1 whole, which is shorter than its diff:
```python
import functools

import jax
import jax.numpy as jnp
from jax import lax
from jax.experimental import pallas as pl
from jax.experimental.pallas import tpu as pltpu
from jax.sharding import PartitionSpec as P

SPAN = 128
eps = 1e-05
F32 = jnp.float32
BF16 = jnp.bfloat16


def silu(u):
    return u * (1.0 / (1.0 + jnp.exp(-u)))


def spread_heads(coef, expand):
    high = coef.astype(BF16)
    low = (coef - high.astype(F32)).astype(BF16)
    return jnp.dot(high, expand, preferred_element_type=F32) + jnp.dot(
        low, expand, preferred_element_type=F32
    )


def conv_cols(buf, cols, taps, marks):
    summed = taps[3:4, :] * buf[8 : 8 + SPAN, cols]
    for back in range(1, 4):
        keep = marks[:, 2 + back : 3 + back]
        summed = summed + (taps[3 - back : 4 - back, :] * buf[8 - back : 8 - back + SPAN, cols]) * keep
    return silu(summed).astype(BF16)


def scan_kernel(pieces, groups, heads, state, width, index_ref, *refs):
    x_refs = refs[:pieces]
    m_refs = refs[pieces : 2 * pieces]
    (rim_x, rim_m, taps_x, taps_m, marks_ref, segrow_ref, cum_ref, rev_ref, carry_ref, reach_ref,
     gate_ref, skip_ref, expand_ref, y_ref, c_ref, slab_ref, xbuf, mbuf, carried) = refs[2 * pieces :]
    block = pl.program_id(0)
    prow = SPAN // pieces
    inner = xbuf.shape[1]
    maps = mbuf.shape[1]

    @pl.when(block == 0)
    def _():
        xbuf[0:8, :] = rim_x[prow - 8 : prow, :].astype(F32)
        mbuf[0:8, :] = rim_m[prow - 8 : prow, :maps].astype(F32)
        carried[...] = jnp.zeros_like(carried)

    @pl.when(block > 0)
    def _():
        xbuf[0:8, :] = xbuf[SPAN : SPAN + 8, :]
        mbuf[0:8, :] = mbuf[SPAN : SPAN + 8, :]

    for k in range(pieces):
        xbuf[8 + k * prow : 8 + (k + 1) * prow, :] = x_refs[k][0].astype(F32)
        mbuf[8 + k * prow : 8 + (k + 1) * prow, :] = m_refs[k][0].astype(F32)
    marks = marks_ref[...]
    seg_t = marks[:, 0:1]
    ti = lax.broadcasted_iota(jnp.int32, (SPAN, SPAN), 0)
    si = lax.broadcasted_iota(jnp.int32, (SPAN, SPAN), 1)
    allowed = (ti >= si) & (seg_t == segrow_ref[0])
    bias = jnp.where(allowed, 0.0, -1e30)
    left = lax.broadcasted_iota(jnp.int32, (SPAN, 2 * width), 1) < width
    cum = cum_ref[...]
    rev = rev_ref[0]
    carry = carry_ref[...]
    reach = reach_ref[...]
    per_group = heads // groups
    for g in range(groups):
        parts = []
        for q in range(2 * state // 128):
            cols = slice(g * 2 * state + q * 128, g * 2 * state + (q + 1) * 128)
            parts.append(conv_cols(mbuf, cols, taps_m[:, cols], marks))
        half = len(parts) // 2
        b_g = jnp.concatenate(parts[:half], axis=1)
        c_g = jnp.concatenate(parts[half:], axis=1)
        c_ref[:, g * state : (g + 1) * state] = c_g
        scores = lax.dot_general(c_g, b_g, (((1,), (1,)), ((), ())), preferred_element_type=F32)
        for p in range(per_group // 2):
            h = g * per_group + 2 * p
            cols = slice(h * width, (h + 2) * width)
            xc = conv_cols(xbuf, cols, taps_x[:, cols], marks)
            weights = []
            for k in (h, h + 1):
                decay = jnp.exp((cum[:, k : k + 1] + rev[k : k + 1, :]) + bias)
                weights.append((decay * scores).astype(BF16))
            zero = jnp.zeros_like(xc)
            both = jnp.concatenate([jnp.where(left, xc, zero), jnp.where(left, zero, xc)], axis=0)
            y = jnp.dot(jnp.concatenate(weights, axis=1), both, preferred_element_type=F32)
            expand = expand_ref[:, cols]
            prior = carried[:, cols]
            off = jnp.dot(c_g, prior.astype(BF16), preferred_element_type=F32)
            xf = xc.astype(F32)
            y_ref[:, cols] = y + off * spread_heads(reach, expand) + skip_ref[:, cols] * xf
            xw = (xf * spread_heads(carry, expand)).astype(BF16)
            added = lax.dot_general(b_g, xw, (((0,), (0,)), ((), ())), preferred_element_type=F32)
            carried[:, cols] = gate_ref[0, :, cols] * prior + added

    @pl.when(block == pl.num_programs(0) - 1)
    def _():
        slab_ref[...] = carried[...].astype(BF16)


def gate_kernel(pieces, groups, heads, state, width, index_ref, *refs):
    z_refs = refs[:pieces]
    y_ref, c_ref, coef_ref, arriving_ref, expand_ref, gain_ref, out_ref, gated, zbuf = refs[pieces:]
    prow = SPAN // pieces
    for k in range(pieces):
        zbuf[k * prow : (k + 1) * prow, :] = z_refs[k][0]
    coef = coef_ref[...]
    inner = heads * width
    size = inner // groups
    for g in range(groups):
        c_g = c_ref[:, g * state : (g + 1) * state]
        total = jnp.zeros((SPAN, 128), F32)
        for q in range(size // 128):
            cols = slice(g * size + q * 128, g * size + (q + 1) * 128)
            off = jnp.dot(c_g, arriving_ref[:, cols], preferred_element_type=F32)
            y = y_ref[:, cols] + off * spread_heads(coef, expand_ref[:, cols])
            value = y * silu(zbuf[:, cols].astype(F32))
            gated[:, q * 128 : (q + 1) * 128] = value
            total = total + value * value
        scale = lax.rsqrt(jnp.sum(total, axis=1, keepdims=True) * (1.0 / size) + eps)
        for q in range(size // 128):
            cols = slice(g * size + q * 128, g * size + (q + 1) * 128)
            out_ref[:, cols] = (
                gated[:, q * 128 : (q + 1) * 128] * scale * gain_ref[:, cols]
            ).astype(BF16)


def passed_along(block, axis, distance):
    devices = range(lax.axis_size(axis))
    route = [(i - distance, i) for i in devices if i - distance in devices]
    return lax.ppermute(block, axis, route)


def body(token_values, gate_values, state_maps, step_raw, log_rate, skip_gain, conv_values, conv_maps,
         piece_shift, doc_start, norm_gain, out_weight):
    owners = lax.axis_size(("dp", "ctx"))
    myself = lax.axis_index(("dp", "ctx"))
    slots = piece_shift.shape[0]
    rows = token_values.shape[1]
    prow = rows // slots
    most = 2 * slots // owners
    inner = token_values.shape[2]
    heads = log_rate.shape[0]
    groups = state_maps.shape[2]
    state = state_maps.shape[3] // 2
    maps = groups * 2 * state
    width = inner // heads
    blocks = rows // SPAN
    pieces = SPAN // prow

    slot_ids = jnp.arange(slots, dtype=jnp.int32)
    matching = piece_shift[:, None] == piece_shift[None, :]
    ranking = jnp.sum((matching & (slot_ids[None, :] < slot_ids[:, None])).astype(jnp.int32), axis=1)
    offsets = (jnp.arange(owners, dtype=jnp.int32) - myself) % owners
    chosen = (piece_shift[None, None, :] == offsets[:, None, None]) & (
        ranking[None, None, :] == jnp.arange(most, dtype=jnp.int32)[None, :, None]
    )
    send_slot = jnp.sum(chosen.astype(jnp.int32) * slot_ids[None, None, :], axis=2)
    source = (myself - piece_shift) % owners
    index = source * most + ranking

    def exchange(local):
        cut = local.reshape(slots, prow, local.shape[-1])
        got = lax.all_to_all(cut[send_slot], ("dp", "ctx"), split_axis=0, concat_axis=0, tiled=True)
        return got.reshape(owners * most, prow, local.shape[-1])

    steps = jnp.pad(step_raw[0], ((0, 0), (0, (-heads) % 128)))
    m_got = exchange(jnp.concatenate([state_maps[0].reshape(rows, maps), steps], axis=1))
    x_got = exchange(token_values[0])
    z_got = exchange(gate_values[0])

    flags = doc_start[0].astype(F32)
    tail = passed_along(flags[rows - 3 :], "ctx", 1)
    free = 1.0 - jnp.concatenate([tail, flags])
    k1 = free[3:]
    k2 = k1 * free[2 : 2 + rows]
    k3 = k2 * free[1 : 1 + rows]
    segment = jnp.cumsum(flags.reshape(blocks, SPAN), axis=1)
    same_end = (segment == segment[:, -1:]).astype(F32)
    first = (segment == 0).astype(F32)
    nil = jnp.zeros((rows,), F32)
    marks = jnp.stack(
        [segment.reshape(rows), same_end.reshape(rows), first.reshape(rows), k1, k2, k3, nil, nil], axis=1
    )

    dt_raw = m_got[index][:, :, maps : maps + heads].reshape(rows, heads)
    dt = jax.nn.softplus(dt_raw.astype(F32)).reshape(blocks, SPAN, heads)
    cum = jnp.cumsum(dt * (-jnp.exp(log_rate)), axis=1)
    rev = (jnp.log(dt) - cum).transpose(0, 2, 1)
    last = cum[:, -1:]
    carry = jnp.exp(last - cum) * dt * same_end[:, :, None]
    reach = jnp.exp(cum) * first[:, :, None]
    gates = jnp.exp(cum[:, -1]) * first[:, -1:]
    before = [jnp.ones((heads,), F32)]
    for b in range(blocks):
        before.append(before[-1] * gates[b])
    coef = reach * jnp.stack(before[:blocks])[:, None, :]
    gate_rows = jnp.repeat(gates, width, axis=1)[:, None, :]
    expand = (
        jnp.arange(heads)[:, None] == jnp.arange(inner)[None, :] // width
    ).astype(BF16)

    rim_m, rim_x = passed_along(
        (m_got[index[slots - 1]], x_got[index[slots - 1]]), "ctx", 1
    )

    def piece_specs(cols):
        return [
            pl.BlockSpec((1, prow, cols), functools.partial(lambda k, b, i: (i[b * pieces + k], 0, 0), k))
            for k in range(pieces)
        ]

    def whole(shape):
        return pl.BlockSpec(shape, lambda b, i: (0,) * len(shape))

    def by_block(cols):
        return pl.BlockSpec((SPAN, cols), lambda b, i: (b, 0))

    lim = 48 * 1024 * 1024
    y_part, c_all, slab = pl.pallas_call(
        functools.partial(scan_kernel, pieces, groups, heads, state, width),
        grid_spec=pltpu.PrefetchScalarGridSpec(
            num_scalar_prefetch=1,
            grid=(blocks,),
            in_specs=piece_specs(inner)
            + piece_specs(maps)
            + [
                whole((prow, inner)),
                whole(rim_m.shape),
                whole((4, inner)),
                whole((4, maps)),
                by_block(8),
                pl.BlockSpec((1, 1, SPAN), lambda b, i: (b, 0, 0)),
                by_block(heads),
                pl.BlockSpec((1, heads, SPAN), lambda b, i: (b, 0, 0)),
                by_block(heads),
                by_block(heads),
                pl.BlockSpec((1, 1, inner), lambda b, i: (b, 0, 0)),
                whole((1, inner)),
                whole((heads, inner)),
            ],
            out_specs=[by_block(inner), by_block(groups * state), whole((state, inner))],
            scratch_shapes=[
                pltpu.VMEM((SPAN + 8, inner), F32),
                pltpu.VMEM((SPAN + 8, maps), F32),
                pltpu.VMEM((state, inner), F32),
            ],
        ),
        out_shape=[
            jax.ShapeDtypeStruct((rows, inner), F32),
            jax.ShapeDtypeStruct((rows, groups * state), BF16),
            jax.ShapeDtypeStruct((state, inner), BF16),
        ],
        compiler_params=pltpu.CompilerParams(vmem_limit_bytes=lim),
        cost_estimate=pl.CostEstimate(flops=4_000_000_000, bytes_accessed=12_000_000, transcendentals=4_000_000),
        name="scan",
    )(
        index,
        *([x_got] * pieces),
        *([m_got] * pieces),
        rim_x,
        rim_m,
        conv_values,
        conv_maps.reshape(4, maps),
        marks,
        segment[:, None, :],
        cum.reshape(rows, heads),
        rev,
        carry.reshape(rows, heads),
        reach.reshape(rows, heads),
        gate_rows,
        jnp.repeat(skip_gain, width)[None, :],
        expand,
    )

    if lax.axis_size("ctx") == 2:
        arriving = passed_along(slab, "ctx", 1)
    else:
        slabs = lax.all_gather(slab, "ctx")
        factors = lax.all_gather(jnp.repeat(before[blocks], width), "ctx")

        def one(turn, total):
            return (
                lax.dynamic_index_in_dim(factors, turn, 0, False)[None, :] * total
                + lax.dynamic_index_in_dim(slabs, turn, 0, False).astype(F32)
            )

        arriving = lax.fori_loop(0, lax.axis_index("ctx"), one, jnp.zeros(slab.shape, F32)).astype(BF16)

    normed = pl.pallas_call(
        functools.partial(gate_kernel, pieces, groups, heads, state, width),
        grid_spec=pltpu.PrefetchScalarGridSpec(
            num_scalar_prefetch=1,
            grid=(blocks,),
            in_specs=piece_specs(inner)
            + [
                by_block(inner),
                by_block(groups * state),
                by_block(heads),
                whole((state, inner)),
                whole((heads, inner)),
                whole((1, inner)),
            ],
            out_specs=by_block(inner),
            scratch_shapes=[pltpu.VMEM((SPAN, inner // groups), F32), pltpu.VMEM((SPAN, inner), BF16)],
        ),
        out_shape=jax.ShapeDtypeStruct((rows, inner), BF16),
        compiler_params=pltpu.CompilerParams(vmem_limit_bytes=lim),
        cost_estimate=pl.CostEstimate(flops=1_000_000_000, bytes_accessed=10_000_000, transcendentals=1_000_000),
        name="gating",
    )(
        index,
        *([z_got] * pieces),
        y_part,
        c_all,
        coef.reshape(rows, heads),
        arriving,
        expand,
        norm_gain[None, :],
    )
    partial_value = jnp.dot(normed, out_weight, preferred_element_type=F32)
    result = lax.psum_scatter(partial_value.astype(BF16), "head", scatter_dimension=1, tiled=True)
    return result[None]


def solution(mesh):
    return jax.shard_map(
        body,
        mesh=mesh,
        in_specs=(
            P("dp", "ctx", "head"),
            P("dp", "ctx", "head"),
            P("dp", "ctx", "head", None),
            P("dp", "ctx", "head"),
            P("head"),
            P("head"),
            P(None, "head"),
            P(None, "head", None),
            P(),
            P("dp", "ctx"),
            P("head"),
            P("head", None),
        ),
        out_specs=P("dp", "ctx", "head"),
        check_vma=False,
    )
```

time: 310 us -> 265 us (0.85)
  other arithmetic: 42.8 us -> 6.4 us
  local copies, waits for them, and re-layouts: 60.8 us -> 27.6 us
  Pallas kernels: 0 us -> 28.1 us
  matrix products: 31.2 us -> 13.8 us
  waiting for transfers between devices: 132 us -> 148 us
    pallas_call x0 -> x2, Pallas kernels: none -> 28.1 us  [the longest x1 21 us: body(): pl.pallas_call(functools.partial(scan_kernel, pieces, groups, heads, stat...]
    all_to_all x4 -> x3, waiting for transfers between devices: 52.3 us -> 72.2 us  [exchange(): lax.all_to_all(cut[send_slot], ('dp', 'ctx'), split_axis=0, concat_axis=0...]
    convert_element_type x10 -> x5, other arithmetic: 19.1 us -> 1.03 us  [the longest x1 0.92 us: body(): dt = jax.nn.softplus(dt_raw.astype(F32)).reshape(blocks, SPAN, heads)]
    dot_general x5 -> x1, matrix products: 31.2 us -> 13.8 us  [body(): partial_value = jnp.dot(normed, out_weight, preferred_element_type=F32)]
    convert_element_type x6 -> x1, local copies, waits for them, and re-layouts: 16.2 us -> 0.1 us  [body(): dt = jax.nn.softplus(dt_raw.astype(F32)).reshape(blocks, SPAN, heads)]
    reshape x2 -> x0, local copies, waits for them, and re-layouts: 13.6 us -> none  [body(): x_blocks = x_conv.reshape(blocks, span, groups_local, per_group, width)]
    add x4 -> x0, other arithmetic: 7.85 us -> none  [advance(): gate_now[:, None, None] * summed + state_now]
    gather x9 -> x4, local copies, waits for them, and re-layouts: 19.8 us -> 12.8 us  [the longest x3 9.35 us: exchange(): cut[send_slot]]
  transfers between devices with their start and end apart: 9 -> 8, of which waited for: 4 -> 4; matrix products, arithmetic and copies ran while one was open for 34% -> 7% of each run, Pallas kernels for 0% -> 8%
where the time goes in v1:
time: 265 us; the launch traced here: 262 us
  waiting for transfers between devices  148 us (56%)
  Pallas kernels  28.1 us (11%)
  local copies, waits for them, and re-layouts  27.6 us (10%)
  starting transfers between devices  21.8 us (8%)
  between operations  15.6 us (6%)
  matrix products  13.8 us (5%)
  other arithmetic  6.4 us (2%)
    reduce_scatter x1, waiting for transfers between devices, body(): lax.psum_scatter(partial_value.astype(BF16), 'head', scatter_dimension=1,...  76.2 us
    all_to_all x3, waiting for transfers between devices, exchange(): lax.all_to_all(cut[send_slot], ('dp', 'ctx'), split_axis=0, concat_axis=0...  72.2 us
    pallas_call x1, Pallas kernels, body(): pl.pallas_call(functools.partial(scan_kernel, pieces, groups, heads, stat...  21 us
    dot_general x1, matrix products, body(): partial_value = jnp.dot(normed, out_weight, preferred_element_type=F32)  13.8 us
    all_to_all x3, starting transfers between devices, exchange(): lax.all_to_all(cut[send_slot], ('dp', 'ctx'), split_axis=0, concat_axis=0...  13.6 us
    gather x3, local copies, waits for them, and re-layouts, exchange(): cut[send_slot]  9.35 us
    ppermute x4, starting transfers between devices, passed_along(): return lax.ppermute(block, axis, route)  8.15 us
    unnamed x32, local copies, waits for them, and re-layouts  8.11 us
  transfers between devices with their start and end apart: 8, of which 4 were waited for; matrix products, arithmetic and copies ran while one was open for 7% of the time, Pallas kernels for 8%

profile of v1, /device:TPU:8, one launch (start us, length us, event | category | flops | bytes accessed | tf_op | source)
XLA Modules:
  0.0 261.8 jit_solution(1933315167944559701)
XLA Ops:
  6.5 1.0 convert_reduce_fusion
  7.6 0.7 iota_compare_fusion.2
  8.3 0.2 select_reduce_fusion
  8.6 0.9 copy.40
  9.5 2.6 concatenate.11
  12.1 1.3 pad_maximum_fusion
  13.4 2.2 gather_fusion.2
  15.6 4.4 %all-to-all-start.2 = ((bf16[8,8,16,1152]{3,2,1,0:T(8,128)(2,1)}), bf16[8,8,16,1152]{3,2,1,0:T(8,128)(2,1)}, u32[]{:S(2)}, u32[]{:S(2)}) async-start(bf16[8,8,16,1152]{3,2,1,0:T(8,128)(2,1)} %bitcast.81), calls=%async_computation.2 | async-start | bytes 4718592 | tf_op jit(solution)/shard_map/all_to_all | solution.py:170
  20.0 2.8 %gather_fusion.1 = bf16[64,16,2048]{2,1,0:T(8,128)(2,1)} fusion(bf16[32,16,2048]{2,1,0:T(8,128)(2,1)S(1)} %bitcast.72, s32[1024]{0:T(1024)S(1)} %pad_clamp_fusion.1), kind=kCustom, calls=%fused_computation.1 | custom fusion | bytes 8388864 | tf_op jit(solution)/shard_map/gather | solution.py:170
  22.8 26.7 %all-to-all-done.2 = bf16[8,8,16,1152]{3,2,1,0:T(8,128)(2,1)} async-done(((bf16[8,8,16,1152]{3,2,1,0:T(8,128)(2,1)}), bf16[8,8,16,1152]{3,2,1,0:T(8,128)(2,1)}, u32[]{:S(2)}, u32[]{:S(2)}) %all-to-all-start.2) | async-done | bytes 2359328 | tf_op jit(solution)/shard_map/all_to_all | solution.py:170
  49.5 4.7 %all-to-all-start.1 = ((bf16[8,8,16,2048]{3,2,1,0:T(8,128)(2,1)}), bf16[8,8,16,2048]{3,2,1,0:T(8,128)(2,1)}, u32[]{:S(2)}, u32[]{:S(2)}) async-start(bf16[8,8,16,2048]{3,2,1,0:T(8,128)(2,1)} %bitcast.80), calls=%async_computation.1 | async-start | bytes 8388608 | tf_op jit(solution)/shard_map/all_to_all | solution.py:170
  54.3 2.3 collective-permute-start.2
  56.6 0.6 slice.42
  58.6 0.6 copy.49
  59.2 4.4 %gather_fusion = bf16[64,16,2048]{2,1,0:T(8,128)(2,1)} fusion(bf16[32,16,2048]{2,1,0:T(8,128)(2,1)} %bitcast.82, s32[1024]{0:T(1024)S(1)} %pad_clamp_fusion.1), kind=kCustom, calls=%fused_computation | custom fusion | bytes 8388864 | tf_op jit(solution)/shard_map/gather | solution.py:170
  64.2 0.3 reduce_window_sum.22
  64.5 0.2 slice_reduce_fusion
  64.8 0.2 convert_reduce_fusion.1
  65.1 38.2 %all-to-all-done.1 = bf16[8,8,16,2048]{3,2,1,0:T(8,128)(2,1)} async-done(((bf16[8,8,16,2048]{3,2,1,0:T(8,128)(2,1)}), bf16[8,8,16,2048]{3,2,1,0:T(8,128)(2,1)}, u32[]{:S(2)}, u32[]{:S(2)}) %all-to-all-start.1) | async-done | bytes 4194336 | tf_op jit(solution)/shard_map/all_to_all | solution.py:170
  103.3 4.6 %all-to-all-start = ((bf16[8,8,16,2048]{3,2,1,0:T(8,128)(2,1)}), bf16[8,8,16,2048]{3,2,1,0:T(8,128)(2,1)}, u32[]{:S(2)}, u32[]{:S(2)}) async-start(bf16[8,8,16,2048]{3,2,1,0:T(8,128)(2,1)} %bitcast.79), calls=%async_computation | async-start | bytes 8388608 | tf_op jit(solution)/shard_map/all_to_all | solution.py:170
  108.2 0.1 copy.48.refs_20_
  108.3 3.4 %gather_fusion.3 = bf16[32,16,1152]{2,1,0:T(8,128)(2,1)} fusion(bf16[64,16,1152]{2,1,0:T(8,128)(2,1)} %bitcast.10.refs_8_.refs_9_.refs_10_.refs_11_.refs_12_.refs_13_.refs_14_.refs_15_, s32[1024]{0:T(1024)S(1)} %pad_clamp_fusion), kind=kCustom, calls=%fused_computation.3 | custom fusion | bytes 2359424 | tf_op jit(solution)/shard_map/gather | solution.py:192
  111.7 0.9 slice_convert_fusion
  112.6 0.1 copy.41
  112.8 0.1 copy.46
  113.0 0.3 reduce_window_sum.23
  113.3 0.8 dynamic-slice_bitcast_fusion.1
  114.1 2.2 collective-permute-start.1
  116.4 0.7 subtract_bitcast_fusion.refs_23_
  117.1 0.8 dynamic-slice_bitcast_fusion
  117.9 1.3 collective-permute-start
  119.4 0.7 broadcast_in_dim_reshape.6.refs_26_
  120.1 0.2 bitcast_multiply_fusion
  120.4 0.6 copy-done.6
  121.0 0.6 copy-done.3
  121.6 0.8 copy-done.1
  122.4 0.8 copy-done.2
  123.2 0.8 copy-done.4
  124.0 0.7 copy-done.5
  124.8 0.8 copy-done.7
  125.5 0.8 copy-done.8
  126.3 21.0 %scan.1 = (f32[512,2048]{1,0:T(8,128)}, bf16[512,512]{1,0:T(8,128)(2,1)S(1)}, bf16[256,2048]{1,0:T(8,128)(2,1)}) custom-call(s32[32]{0:T(128)S(1)} %get-tuple-element.18.index_ref, bf16[64,16,2048]{2,1,0:T(8,128)(2,1)} %bitcast.6.refs_0_.refs_1_.refs_2_.refs_3_.refs_4_.refs_5_.refs_6_.refs_7_, ...), custom_call_target="tpu_custom_call" | custom-call | flops 4000000000 | bytes 12000000 | tf_op jit(solution)/shard_map/scan/pallas_call | solution.py:226
  147.3 2.4 collective-permute-start.3
  149.6 7.4 %all-to-all-done = bf16[8,8,16,2048]{3,2,1,0:T(8,128)(2,1)} async-done(((bf16[8,8,16,2048]{3,2,1,0:T(8,128)(2,1)}), bf16[8,8,16,2048]{3,2,1,0:T(8,128)(2,1)}, u32[]{:S(2)}, u32[]{:S(2)}) %all-to-all-start) | async-done | bytes 4194336 | tf_op jit(solution)/shard_map/all_to_all | solution.py:170
  157.0 0.7 copy-done.9
  157.7 7.2 %gating.1 = bf16[512,2048]{1,0:T(8,128)(2,1)S(1)} custom-call(s32[32]{0:T(128)S(1)} %get-tuple-element.18.index_ref, bf16[64,16,2048]{2,1,0:T(8,128)(2,1)} %bitcast.3.refs_0_.refs_1_.refs_2_.refs_3_.refs_4_.refs_5_.refs_6_.refs_7_, bf16[64,16,2048]{2,1,0:T(8,128)(2,1)} %bitcast.3.refs_0_.refs_1_.refs_2_.refs_3_.refs_4_.refs_5_.refs_6_.refs_7_, ...), custom_call_target="tpu_custom_call" | custom-call | flops 1000000000 | bytes 10000000 | tf_op jit(solution)/shard_map/gating/pallas_call | solution.py:296
  164.9 13.8 %convolution_convert_fusion = bf16[512,4096]{1,0:T(8,128)(2,1)} fusion(bf16[512,2048]{1,0:T(8,128)(2,1)S(1)} %gating.1, bf16[2048,4096]{1,0:T(8,128)(2,1)} %param.23), kind=kOutput, calls=%fused_computation.4 | convolution fusion | flops 8592031744 | bytes 23068672 | tf_op jit(solution)/shard_map/dot_general | solution.py:327
  178.8 76.2 %reduce-scatter.2.cloned.1.call-done = bf16[512,1024]{1,0:T(8,128)(2,1)} async-done(((bf16[512,4096]{1,0:T(8,128)(2,1)}), bf16[512,1024]{1,0:T(8,128)(2,1)}) %reduce-scatter.2.cloned.1.call-update) | async-done | bytes 1048592 | tf_op jit(solution)/shard_map/reduce_scatter | solution.py:328
  (56 shorter events, 1.3 us)
Async XLA Ops:
  6.5 13.5 %copy-start = (bf16[1,512,2048]{2,1,0:T(8,128)(2,1)S(1)}, bf16[1,512,2048]{2,1,0:T(8,128)(2,1)}, u32[]{:S(2)}) copy-start(bf16[1,512,2048]{2,1,0:T(8,128)(2,1)} %param.12) | copy-start | bytes 6291460
  15.6 33.8 %all-to-all-start.2 = ((bf16[8,8,16,1152]{3,2,1,0:T(8,128)(2,1)}), bf16[8,8,16,1152]{3,2,1,0:T(8,128)(2,1)}, u32[]{:S(2)}, u32[]{:S(2)}) async-start(bf16[8,8,16,1152]{3,2,1,0:T(8,128)(2,1)} %bitcast.81), calls=%async_computation.2 | async-start | bytes 4718592 | tf_op jit(solution)/shard_map/all_to_all | solution.py:170
  49.5 4.7 %copy-start.12 = (s32[1,512]{1,0:T(1,128)S(1)}, s32[1,512]{1,0:T(1,128)}, u32[]{:S(2)}) copy-start(s32[1,512]{1,0:T(1,128)} %param.21) | copy-start | bytes 6148
  49.5 7.1 %copy-start.11 = (s32[32]{0:T(128)S(1)}, s32[32]{0:T(128)}, u32[]{:S(2)}) copy-start(s32[32]{0:T(128)} %param.20) | copy-start | bytes 388
  49.5 9.0 %copy-start.13 = (f32[32]{0:T(128)S(1)}, f32[32]{0:T(128)}, u32[]{:S(2)}) copy-start(f32[32]{0:T(128)} %param.17) | copy-start | bytes 388
  49.5 9.1 %copy-start.10 = (f32[4,2,512]{2,1,0:T(2,128)S(1)}, f32[4,2,512]{2,1,0:T(2,128)}, u32[]{:S(2)}) copy-start(f32[4,2,512]{2,1,0:T(2,128)} %param.19) | copy-start | bytes 49156
  49.5 53.8 %all-to-all-start.1 = ((bf16[8,8,16,2048]{3,2,1,0:T(8,128)(2,1)}), bf16[8,8,16,2048]{3,2,1,0:T(8,128)(2,1)}, u32[]{:S(2)}, u32[]{:S(2)}) async-start(bf16[8,8,16,2048]{3,2,1,0:T(8,128)(2,1)} %bitcast.80), calls=%async_computation.1 | async-start | bytes 8388608 | tf_op jit(solution)/shard_map/all_to_all | solution.py:170
  54.3 53.7 %collective-permute-start.2 = (f32[3]{0:T(128)S(1)}, f32[3]{0:T(128)S(1)}, u32[]{:S(2)}, u32[]{:S(2)}) collective-permute-start(f32[3]{0:T(128)S(1)} %slice_bitcast_fusion), channel_id=1, source_target_pairs={{0,4},{1,5},{2,6},{3,7},{8,12},{9,13},{10,14},{11,15},{16,20},{17,... | collective-permute-start | bytes 44 | tf_op jit(solution)/shard_map/ppermute | solution.py:137
  59.2 5.8 %copy-start.14 = (f32[32]{0:T(128)S(1)}, f32[32]{0:T(128)}, u32[]{:S(2)}) copy-start(f32[32]{0:T(128)} %param.16) | copy-start | bytes 388
  103.3 53.7 %all-to-all-start = ((bf16[8,8,16,2048]{3,2,1,0:T(8,128)(2,1)}), bf16[8,8,16,2048]{3,2,1,0:T(8,128)(2,1)}, u32[]{:S(2)}, u32[]{:S(2)}) async-start(bf16[8,8,16,2048]{3,2,1,0:T(8,128)(2,1)} %bitcast.79), calls=%async_computation | async-start | bytes 8388608 | tf_op jit(solution)/shard_map/all_to_all | solution.py:170
  107.9 147.1 %reduce-scatter.2.cloned.1.call-start = ((), (), s32[]{:S(2)}) async-start(), calls=%async_computation.4 | async-start | bytes 5242880 | tf_op jit(solution)/shard_map/reduce_scatter | solution.py:328
  114.1 6.2 %collective-permute-start.1 = (bf16[16,1152]{1,0:T(8,128)(2,1)S(1)}, bf16[16,1152]{1,0:T(8,128)(2,1)S(1)}, u32[]{:S(2)}, u32[]{:S(2)}) collective-permute-start(bf16[16,1152]{1,0:T(8,128)(2,1)S(1)} %dynamic-slice_bitcast_fusion.1), channel_id=1, source_target_pairs={{0,4},{1,5},{2,6},{3,7},{8,12},{9,13},{10,14},{11,15},{16,20},{17,... | collective-permute-start | bytes 110600 | tf_op jit(solution)/shard_map/ppermute | solution.py:137
  117.9 3.0 %collective-permute-start = (bf16[16,2048]{1,0:T(8,128)(2,1)S(1)}, bf16[16,2048]{1,0:T(8,128)(2,1)S(1)}, u32[]{:S(2)}, u32[]{:S(2)}) collective-permute-start(bf16[16,2048]{1,0:T(8,128)(2,1)S(1)} %dynamic-slice_bitcast_fusion), channel_id=1, source_target_pairs={{0,4},{1,5},{2,6},{3,7},{8,12},{9,13},{10,14},{11,15},{16,20},{17,... | collective-permute-start | bytes 196616 | tf_op jit(solution)/shard_map/ppermute | solution.py:137
  120.4 0.6 copy-start.6
  121.0 0.6 copy-start.3
  121.6 0.8 copy-start.1
  122.4 0.8 copy-start.2
  123.2 0.8 copy-start.4
  124.0 0.7 copy-start.5
  124.8 0.8 copy-start.7
  125.5 0.8 copy-start.8
  147.3 9.8 %collective-permute-start.3 = (bf16[256,2048]{1,0:T(8,128)(2,1)}, bf16[256,2048]{1,0:T(8,128)(2,1)}, u32[]{:S(2)}, u32[]{:S(2)}) collective-permute-start(bf16[256,2048]{1,0:T(8,128)(2,1)} %get-tuple-element.10), channel_id=1, source_target_pairs={{0,4},{1,5},{2,6},{3,7},{8,12},{9,13},{10,14},{11,15},{16,20},{17,... | collective-permute-start | bytes 3145736 | tf_op jit(solution)/shard_map/ppermute | solution.py:137
  157.0 0.7 copy-start.9
Sparse Core Ops, SparseCore 0:
  178.9 76.0 reduce-scatter.1
